TPU v7x, 1024 devices: a whole 4x4x32 slice. The times are simulated.
1024 devices in a mesh: gx: 8 (over z_lo), gy: 16 (over y, z_hi), gz: 8 (over x, core).
Axes of the slice: x: 4, y: 4, z: 32 (z_hi: 4, z_lo: 8; z = z_hi * 8 + z_lo), core: 2. Of those that a mesh axis runs over, the one named last changes fastest.
Arguments:
- fine_residual: bfloat16 [8, 16, 8, 2, 2, 12, 32, 256], P('gx', 'gy', 'gz'), may hold values from -6 to 6
- candidates: bfloat16 [8, 16, 8, 2, 48, 2, 12, 256], P('gx', 'gy', 'gz'), may hold values from -0.29882812 to 0.29882812
- vector_pick: int32 [32], replicated, may hold values from 0 to 47, as said below
- coarse_links: float32 [8, 16, 8, 2, 9, 64, 128], P(None, 'gy', 'gz'), may hold values from -0.1875 to 0.1875
Outputs:
- correction: bfloat16 [8, 16, 8, 2, 2, 12, 32, 256], P('gx', 'gy', 'gz')
- coarse_error: float32 [8, 16, 8, 2, 2, 64, 32], P('gx', 'gy', 'gz')
Inputs may be any that keep to these rules, and one draw needn't show every extreme that they name: `vector_pick`: 32 distinct indices of candidate vectors.
All inputs are finite; a program needn't handle non-finite values.
Results may differ from a plain program's by a relative error of at most 0.0049.
Values sent between devices are 32-bit elements; how exact they have to be, the bound alone decides.
A program may use at most 32 MiB of HBM per device.

v0:
```python
import jax
import jax.numpy as jnp
from jax import lax
from jax.sharding import PartitionSpec as P

APPLIES = 2


def extended(shard, sides, width):
    for axis, dim in sides:
        devices, length = (lax.axis_size(axis), shard.shape[dim])
        up = [(i, (i + 1) % devices) for i in range(devices)]
        down = [(j, i) for i, j in up]
        last = lax.slice_in_dim(shard, length - width, length, axis=dim)
        initial = lax.slice_in_dim(shard, 0, width, axis=dim)
        before = lax.ppermute(last, axis, up)
        after = lax.ppermute(initial, axis, down)
        shard = jnp.concatenate([before, shard, after], axis=dim)
    return shard


def restrict_local(chosen, fine_part):
    shaped = chosen.reshape(
        (chosen.shape[0], chosen.shape[1], 2, 2, chosen.shape[3] // 2, chosen.shape[4])
    )
    source = fine_part.reshape(
        (fine_part.shape[0], 2, 2, fine_part.shape[2] // 2, fine_part.shape[3], fine_part.shape[4])
    )
    partial_terms = jnp.einsum(
        "tkqhcs,tphcrs->thkqpr", shaped, source, preferred_element_type=jnp.float32
    )
    real_part = partial_terms[:, :, :, 0, 0] + partial_terms[:, :, :, 1, 1]
    imag_part = partial_terms[:, :, :, 0, 1] - partial_terms[:, :, :, 1, 0]
    merged_shape = (real_part.shape[0], real_part.shape[1] * real_part.shape[2], real_part.shape[3])
    return jnp.stack([real_part.reshape(merged_shape), imag_part.reshape(merged_shape)], axis=1)


def prolong_local(chosen, error_half):
    shaped = chosen.reshape(
        (chosen.shape[0], chosen.shape[1], 2, 2, chosen.shape[3] // 2, chosen.shape[4])
    )
    coarse = error_half.reshape(
        (error_half.shape[0], 2, 2, error_half.shape[2] // 2, error_half.shape[3])
    )
    grid = jnp.einsum("tkqhcs,tphkr->tqphcrs", shaped, coarse, preferred_element_type=jnp.float32)
    real_part = grid[:, 0, 0] - grid[:, 1, 1]
    imag_part = grid[:, 0, 1] + grid[:, 1, 0]
    merged_shape = (real_part.shape[0], chosen.shape[3], real_part.shape[3], real_part.shape[4])
    stacked = jnp.stack([real_part.reshape(merged_shape), imag_part.reshape(merged_shape)], axis=1)
    return stacked.astype(jnp.bfloat16)


def neighbours(iterate, padded):
    shifted = [iterate, jnp.roll(iterate, -1, 0), jnp.roll(iterate, 1, 0)]
    shifted = shifted + [
        padded[:, 2:, 1:-1],
        padded[:, :-2, 1:-1],
        padded[:, 1:-1, 2:],
        padded[:, 1:-1, :-2],
    ]
    shifted = shifted + [jnp.roll(iterate, -1, 3), jnp.roll(iterate, 1, 3)]
    return shifted


def apply_operator(local_links, shifted):
    stacked = jnp.stack([shifted[0]] + [-vector for vector in shifted[1:]], axis=4)
    real_part = stacked[:, :, :, :, :, 0]
    imag_part = stacked[:, :, :, :, :, 1]
    columns = jnp.concatenate(
        [
            jnp.concatenate([real_part, -imag_part], axis=-2),
            jnp.concatenate([imag_part, real_part], axis=-2),
        ],
        axis=-1,
    )
    product = jnp.einsum(
        "abcdeij,abcdejr->abcdir",
        local_links,
        columns,
        precision=lax.Precision.HIGHEST,
        preferred_element_type=jnp.float32,
    )
    split_at = real_part.shape[-1]
    return shifted[0] + jnp.stack([product[..., :split_at], product[..., split_at:]], axis=4)


def on_device(fine_residual, candidates, vector_pick, coarse_links):
    chosen = jnp.take(candidates[0, 0, 0], vector_pick, axis=1)
    restricted = restrict_local(chosen, fine_residual[0, 0, 0])[None, None, None]
    line_source = lax.all_to_all(restricted, "gx", split_axis=6, concat_axis=0, tiled=True)
    iterate = 0.5 * line_source
    for repeat in range(APPLIES):
        padded = extended(iterate, (("gy", 1), ("gz", 2)), 1)
        image = apply_operator(coarse_links, neighbours(iterate, padded))
        iterate = iterate + 0.5 * (line_source - image)
    coarse_error = lax.all_to_all(iterate, "gx", split_axis=0, concat_axis=6, tiled=True)
    error_half = coarse_error[0, 0, 0].astype(jnp.bfloat16)
    correction = prolong_local(chosen, error_half)[None, None, None]
    return (correction, coarse_error)


def solution(mesh):
    placed = (
        P("gx", "gy", "gz", None, None, None, None, None),
        P("gx", "gy", "gz", None, None, None, None, None),
        P(),
        P(None, "gy", "gz", None, None, None, None),
    )
    return jax.shard_map(
        on_device,
        mesh=mesh,
        in_specs=placed,
        out_specs=(
            P("gx", "gy", "gz", None, None, None, None, None),
            P("gx", "gy", "gz", None, None, None, None),
        ),
        check_vma=False,
    )
```

profile of v0, /device:TPU:1, one launch (start us, length us, event | category | flops | bytes accessed | tf_op | source)
XLA Modules:
  0.0 134.9 jit_solution(14259497225421947463)
XLA Ops:
  0.6 0.0 copy-start
  0.6 0.8 compare_and_fusion
  1.4 0.7 compare_select_fusion
  2.1 0.0 copy-done
  2.1 2.1 %gather_fusion = bf16[32,2,2,12,256]{4,2,3,1,0:T(2,128)(2,1)S(1)} fusion(bf16[2,48,2,12,256]{4,2,3,1,0:T(2,128)(2,1)S(1)} %bitcast.188, s32[1024]{0:T(1024)S(1)} %pad_clamp_fusion), kind=kCustom, calls=%fused_computation | custom fusion | bytes 1572992 | tf_op jit(solution)/shard_map/jit(_take)/gather | solution.py:88
  4.2 1.9 %convolution_bitcast_fusion.1 = f32[2,2,32,2,2,32]{5,2,4,3,1,0:T(8,128)S(1)} fusion(bf16[2,2,2,6,32,256,1]{5,4,3,2,1,0,6:T(8,128)(2,1)} %bitcast.210, bf16[2,32,2,2,6,256]{5,2,4,3,0,1:T(2,128)(2,1)S(1)} %bitcast.189, pred[32]{0:T(512)(128)(4,1)S(1)} %compare_and_fusion), kind=kOutput, calls=%fused_computation.6 | convolution fusion | flops 50724864 | bytes 1638432 | tf_op jit(solution)/shard_map/tkqhcs,tphcrs->thkqpr/dot_general | solution.py:29
  6.2 0.1 copy.149
  6.3 0.1 copy.150
  6.3 0.1 fusion.45
  6.4 0.1 reshape.628
  6.5 22.4 %all_to_all.39 = f32[8,1,1024]{2,1,0:T(1,128)S(1)} all-to-all(f32[8,1,1024]{2,1,0:T(1,128)S(1)} %reshape.628), channel_id=1, replica_groups=mesh['gx'=8,'gy'=16,'gz'=8] {'gx'}, dimensions={0} | all-to-all | bytes 65536 | tf_op jit(solution)/shard_map/all_to_all | solution.py:90
  28.9 0.5 broadcast.82
  29.4 0.7 reduce
  30.1 0.1 reshape.629
  30.2 0.0 copy-start.1
  30.3 15.7 %collective-permute-start.1 = (f32[8,1,1,2,2,64,4]{5,0,6,4,3,2,1:T(8,128)S(1)}, f32[8,1,1,2,2,64,4]{5,0,6,4,3,2,1:T(8,128)S(1)}, u32[]{:S(2)}, u32[]{:S(2)}) collective-permute-start(f32[8,1,1,2,2,64,4]{5,0,6,4,3,2,1:T(8,128)S(1)} %bitcast_multiply_fusion), channel_id=1, source_target_pairs={{0,8},{8,16},{16,24},{24,32},{32,40},{40,48},{48,56},{56,64},{64,7... | collective-permute-start | bytes 98312 | tf_op jit(solution)/shard_map/ppermute | solution.py:16
  46.0 4.1 %collective-permute-start = (f32[8,1,1,2,2,64,4]{5,0,6,4,3,2,1:T(8,128)S(1)}, f32[8,1,1,2,2,64,4]{5,0,6,4,3,2,1:T(8,128)S(1)}, u32[]{:S(2)}, u32[]{:S(2)}) collective-permute-start(f32[8,1,1,2,2,64,4]{5,0,6,4,3,2,1:T(8,128)S(1)} %bitcast_multiply_fusion), channel_id=1, source_target_pairs={{8,0},{16,8},{24,16},{32,24},{40,32},{48,40},{56,48},{64,56},{72,6... | collective-permute-start | bytes 98312 | tf_op jit(solution)/shard_map/ppermute | solution.py:17
  50.3 0.0 collective-permute-done.1
  50.4 20.0 %collective-permute-done = f32[8,1,1,2,2,64,4]{5,0,6,4,3,2,1:T(8,128)S(1)} collective-permute-done((f32[8,1,1,2,2,64,4]{5,0,6,4,3,2,1:T(8,128)S(1)}, f32[8,1,1,2,2,64,4]{5,0,6,4,3,2,1:T(8,128)S(1)}, u32[]{:S(2)}, u32[]{:S(2)}) %collective-permute-start) | collective-permute-done | bytes 32800 | tf_op jit(solution)/shard_map/ppermute | solution.py:17
  70.3 1.6 %collective-permute-start.3 = (f32[8,3,1,2,2,64,4]{5,0,6,4,3,2,1:T(8,128)S(1)}, f32[8,3,1,2,2,64,4]{5,0,6,4,3,2,1:T(8,128)S(1)}, u32[]{:S(2)}, u32[]{:S(2)}) collective-permute-start(f32[8,3,1,2,2,64,4]{5,0,6,4,3,2,1:T(8,128)S(1)} %pad_maximum_fusion.1), channel_id=1, source_target_pairs={{0,1},{1,2},{2,3},{3,4},{4,5},{5,6},{6,7},{7,0},{8,9},{9,10},{10,1... | collective-permute-start | bytes 294920 | tf_op jit(solution)/shard_map/ppermute | solution.py:16
  71.9 0.0 collective-permute-start.2
  72.0 5.1 %collective-permute-done.2 = f32[8,3,1,2,2,64,4]{5,0,6,4,3,2,1:T(8,128)S(1)} collective-permute-done((f32[8,3,1,2,2,64,4]{5,0,6,4,3,2,1:T(8,128)S(1)}, f32[8,3,1,2,2,64,4]{5,0,6,4,3,2,1:T(8,128)S(1)}, u32[]{:S(2)}, u32[]{:S(2)}) %collective-permute-start.2) | collective-permute-done | bytes 98336 | tf_op jit(solution)/shard_map/ppermute | solution.py:17
  77.0 0.0 collective-permute-done.3
  77.2 0.2 maximum_bitcast_fusion
  77.4 0.0 copy-done.1
  77.4 4.4 %fusion.4 = f32[8,2,8,64]{3,2,1,0:T(8,128)S(1)} fusion(f32[8,1,1,2,9,64,128]{6,5,4,3,2,1,0:T(8,128)S(1)} %copy-done.1, f32[8,2,9,128,8]{3,0,4,1,2:T(8,128)S(1)} %maximum_bitcast_fusion), kind=kOutput, calls=%fused_computation.7 | convolution fusion | flops 113246208 | bytes 5341184 | tf_op jit(solution)/shard_map/abcdeij,abcdejr->abcdir/dot_general | solution.py:76
  82.0 6.3 %collective-permute-start.4 = (f32[8,1,1,2,2,64,4]{5,0,6,3,4,2,1:T(8,128)S(1)}, f32[8,1,1,2,2,64,4]{5,0,6,3,4,2,1:T(8,128)S(1)}, u32[]{:S(2)}, u32[]{:S(2)}) collective-permute-start(f32[8,1,1,2,2,64,4]{5,0,6,3,4,2,1:T(8,128)S(1)} %copy.167), channel_id=1, source_target_pairs={{8,0},{16,8},{24,16},{32,24},{40,32},{48,40},{56,48},{64,56},{72,6... | collective-permute-start | bytes 98312 | tf_op jit(solution)/shard_map/ppermute | solution.py:17
  88.3 7.7 %collective-permute-start.5 = (f32[8,1,1,2,2,64,4]{5,0,6,3,4,2,1:T(8,128)S(1)}, f32[8,1,1,2,2,64,4]{5,0,6,3,4,2,1:T(8,128)S(1)}, u32[]{:S(2)}, u32[]{:S(2)}) collective-permute-start(f32[8,1,1,2,2,64,4]{5,0,6,3,4,2,1:T(8,128)S(1)} %copy.167), channel_id=1, source_target_pairs={{0,8},{8,16},{16,24},{24,32},{32,40},{40,48},{48,56},{56,64},{64,7... | collective-permute-start | bytes 98312 | tf_op jit(solution)/shard_map/ppermute | solution.py:16
  96.2 8.0 %collective-permute-done.5 = f32[8,1,1,2,2,64,4]{5,0,6,3,4,2,1:T(8,128)S(1)} collective-permute-done((f32[8,1,1,2,2,64,4]{5,0,6,3,4,2,1:T(8,128)S(1)}, f32[8,1,1,2,2,64,4]{5,0,6,3,4,2,1:T(8,128)S(1)}, u32[]{:S(2)}, u32[]{:S(2)}) %collective-permute-start.5) | collective-permute-done | bytes 32800 | tf_op jit(solution)/shard_map/ppermute | solution.py:16
  104.2 0.0 collective-permute-done.4
  104.2 1.8 %collective-permute-start.7 = (f32[8,3,1,2,2,64,4]{5,0,6,3,4,2,1:T(8,128)S(1)}, f32[8,3,1,2,2,64,4]{5,0,6,3,4,2,1:T(8,128)S(1)}, u32[]{:S(2)}, u32[]{:S(2)}) collective-permute-start(f32[8,3,1,2,2,64,4]{5,0,6,3,4,2,1:T(8,128)S(1)} %constant_dynamic-update-slice_fusion), channel_id=1, source_target_pairs={{0,1},{1,2},{2,3},{3,4},{4,5},{5,6},{6,7},{7,0},{8,9},{9,10},{10,1... | collective-permute-start | bytes 294920 | tf_op jit(solution)/shard_map/ppermute | solution.py:16
  106.1 0.0 collective-permute-start.6
  106.1 5.4 %collective-permute-done.6 = f32[8,3,1,2,2,64,4]{5,0,6,3,4,2,1:T(8,128)S(1)} collective-permute-done((f32[8,3,1,2,2,64,4]{5,0,6,3,4,2,1:T(8,128)S(1)}, f32[8,3,1,2,2,64,4]{5,0,6,3,4,2,1:T(8,128)S(1)}, u32[]{:S(2)}, u32[]{:S(2)}) %collective-permute-start.6) | collective-permute-done | bytes 98336 | tf_op jit(solution)/shard_map/ppermute | solution.py:17
  111.5 0.0 collective-permute-done.7
  111.6 0.2 maximum_bitcast_fusion.1
  111.8 4.4 %fusion.7 = f32[8,2,8,64]{3,2,1,0:T(8,128)S(1)} fusion(f32[8,1,1,2,9,64,128]{6,5,4,3,2,1,0:T(8,128)S(1)} %copy-done.1, f32[8,2,9,128,8]{3,0,4,1,2:T(8,128)S(1)} %maximum_bitcast_fusion.1), kind=kOutput, calls=%fused_computation.8 | convolution fusion | flops 113246208 | bytes 5341184 | tf_op jit(solution)/shard_map/abcdeij,abcdejr->abcdir/dot_general | solution.py:76
  116.3 0.1 fusion.34
  116.4 0.1 reshape.630
  116.5 14.8 %all_to_all.40 = f32[8,1,1024]{2,1,0:T(1,128)S(1)} all-to-all(f32[8,1,1024]{2,1,0:T(1,128)S(1)} %reshape.630), channel_id=1, replica_groups=mesh['gx'=8,'gy'=16,'gz'=8] {'gx'}, dimensions={0} | all-to-all | bytes 65536 | tf_op jit(solution)/shard_map/all_to_all | solution.py:96
  131.3 0.7 reduce.1
  132.0 0.1 reshape.631
  132.2 0.6 copy.183
  132.8 0.1 convert_element_type.16
  132.9 0.7 convolution_bitcast_fusion
  133.7 0.3 fusion.11
  134.0 1.0 pad_maximum_fusion
  (48 shorter events, 0.8 us)
Async XLA Ops:
  0.6 1.4 %copy-start = (bf16[1,1,1,2,48,2,12,256]{7,5,6,4,3,2,1,0:T(2,128)(2,1)S(1)}, bf16[1,1,1,2,48,2,12,256]{7,5,6,4,3,2,1,0:T(2,128)(2,1)}, u32[]{:S(2)}) copy-start(bf16[1,1,1,2,48,2,12,256]{7,5,6,4,3,2,1,0:T(2,128)(2,1)} %param.5) | copy-start | bytes 3538948
  30.2 47.2 %copy-start.1 = (f32[8,1,1,2,9,64,128]{6,5,4,3,2,1,0:T(8,128)S(1)}, f32[8,1,1,2,9,64,128]{6,5,4,3,2,1,0:T(8,128)}, u32[]{:S(2)}) copy-start(f32[8,1,1,2,9,64,128]{6,5,4,3,2,1,0:T(8,128)} %param.7) | copy-start | bytes 14155780
  30.3 20.0 %collective-permute-start.1 = (f32[8,1,1,2,2,64,4]{5,0,6,4,3,2,1:T(8,128)S(1)}, f32[8,1,1,2,2,64,4]{5,0,6,4,3,2,1:T(8,128)S(1)}, u32[]{:S(2)}, u32[]{:S(2)}) collective-permute-start(f32[8,1,1,2,2,64,4]{5,0,6,4,3,2,1:T(8,128)S(1)} %bitcast_multiply_fusion), channel_id=1, source_target_pairs={{0,8},{8,16},{16,24},{24,32},{32,40},{40,48},{48,56},{56,64},{64,7... | collective-permute-start | bytes 98312 | tf_op jit(solution)/shard_map/ppermute | solution.py:16
  46.0 24.3 %collective-permute-start = (f32[8,1,1,2,2,64,4]{5,0,6,4,3,2,1:T(8,128)S(1)}, f32[8,1,1,2,2,64,4]{5,0,6,4,3,2,1:T(8,128)S(1)}, u32[]{:S(2)}, u32[]{:S(2)}) collective-permute-start(f32[8,1,1,2,2,64,4]{5,0,6,4,3,2,1:T(8,128)S(1)} %bitcast_multiply_fusion), channel_id=1, source_target_pairs={{8,0},{16,8},{24,16},{32,24},{40,32},{48,40},{56,48},{64,56},{72,6... | collective-permute-start | bytes 98312 | tf_op jit(solution)/shard_map/ppermute | solution.py:17
  70.3 6.7 %collective-permute-start.3 = (f32[8,3,1,2,2,64,4]{5,0,6,4,3,2,1:T(8,128)S(1)}, f32[8,3,1,2,2,64,4]{5,0,6,4,3,2,1:T(8,128)S(1)}, u32[]{:S(2)}, u32[]{:S(2)}) collective-permute-start(f32[8,3,1,2,2,64,4]{5,0,6,4,3,2,1:T(8,128)S(1)} %pad_maximum_fusion.1), channel_id=1, source_target_pairs={{0,1},{1,2},{2,3},{3,4},{4,5},{5,6},{6,7},{7,0},{8,9},{9,10},{10,1... | collective-permute-start | bytes 294920 | tf_op jit(solution)/shard_map/ppermute | solution.py:16
  71.9 5.1 %collective-permute-start.2 = (f32[8,3,1,2,2,64,4]{5,0,6,4,3,2,1:T(8,128)S(1)}, f32[8,3,1,2,2,64,4]{5,0,6,4,3,2,1:T(8,128)S(1)}, u32[]{:S(2)}, u32[]{:S(2)}) collective-permute-start(f32[8,3,1,2,2,64,4]{5,0,6,4,3,2,1:T(8,128)S(1)} %pad_maximum_fusion.1), channel_id=1, source_target_pairs={{1,0},{2,1},{3,2},{4,3},{5,4},{6,5},{7,6},{0,7},{9,8},{10,9},{11,1... | collective-permute-start | bytes 294920 | tf_op jit(solution)/shard_map/ppermute | solution.py:17
  82.0 22.2 %collective-permute-start.4 = (f32[8,1,1,2,2,64,4]{5,0,6,3,4,2,1:T(8,128)S(1)}, f32[8,1,1,2,2,64,4]{5,0,6,3,4,2,1:T(8,128)S(1)}, u32[]{:S(2)}, u32[]{:S(2)}) collective-permute-start(f32[8,1,1,2,2,64,4]{5,0,6,3,4,2,1:T(8,128)S(1)} %copy.167), channel_id=1, source_target_pairs={{8,0},{16,8},{24,16},{32,24},{40,32},{48,40},{56,48},{64,56},{72,6... | collective-permute-start | bytes 98312 | tf_op jit(solution)/shard_map/ppermute | solution.py:17
  88.3 15.9 %collective-permute-start.5 = (f32[8,1,1,2,2,64,4]{5,0,6,3,4,2,1:T(8,128)S(1)}, f32[8,1,1,2,2,64,4]{5,0,6,3,4,2,1:T(8,128)S(1)}, u32[]{:S(2)}, u32[]{:S(2)}) collective-permute-start(f32[8,1,1,2,2,64,4]{5,0,6,3,4,2,1:T(8,128)S(1)} %copy.167), channel_id=1, source_target_pairs={{0,8},{8,16},{16,24},{24,32},{32,40},{40,48},{48,56},{56,64},{64,7... | collective-permute-start | bytes 98312 | tf_op jit(solution)/shard_map/ppermute | solution.py:16
  104.2 7.2 %collective-permute-start.7 = (f32[8,3,1,2,2,64,4]{5,0,6,3,4,2,1:T(8,128)S(1)}, f32[8,3,1,2,2,64,4]{5,0,6,3,4,2,1:T(8,128)S(1)}, u32[]{:S(2)}, u32[]{:S(2)}) collective-permute-start(f32[8,3,1,2,2,64,4]{5,0,6,3,4,2,1:T(8,128)S(1)} %constant_dynamic-update-slice_fusion), channel_id=1, source_target_pairs={{0,1},{1,2},{2,3},{3,4},{4,5},{5,6},{6,7},{7,0},{8,9},{9,10},{10,1... | collective-permute-start | bytes 294920 | tf_op jit(solution)/shard_map/ppermute | solution.py:16
  106.1 5.4 %collective-permute-start.6 = (f32[8,3,1,2,2,64,4]{5,0,6,3,4,2,1:T(8,128)S(1)}, f32[8,3,1,2,2,64,4]{5,0,6,3,4,2,1:T(8,128)S(1)}, u32[]{:S(2)}, u32[]{:S(2)}) collective-permute-start(f32[8,3,1,2,2,64,4]{5,0,6,3,4,2,1:T(8,128)S(1)} %constant_dynamic-update-slice_fusion), channel_id=1, source_target_pairs={{1,0},{2,1},{3,2},{4,3},{5,4},{6,5},{7,6},{0,7},{9,8},{10,9},{11,1... | collective-permute-start | bytes 294920 | tf_op jit(solution)/shard_map/ppermute | solution.py:17
where the time goes:
time: 135 us
  waiting for transfers between devices  38.4 us (28%)
  starting transfers between devices  37.3 us (28%)
  blocking collectives  37.2 us (28%)
  matrix products  11.5 us (9%)
  other arithmetic  5.16 us (4%)
  local copies, waits for them, and re-layouts  4.27 us (3%)
    ppermute x4, waiting for transfers between devices, extended(): after = lax.ppermute(initial, axis, down)  30.4 us
    ppermute x4, starting transfers between devices, extended(): before = lax.ppermute(last, axis, up)  26.9 us
    all_to_all x1, blocking collectives, on_device(): lax.all_to_all(restricted, 'gx', split_axis=6, concat_axis=0, tiled=True)  22.4 us
    all_to_all x1, blocking collectives, on_device(): lax.all_to_all(iterate, 'gx', split_axis=0, concat_axis=6, tiled=True)  14.8 us
    ppermute x4, starting transfers between devices, extended(): after = lax.ppermute(initial, axis, down)  10.4 us
    dot_general x2, matrix products, apply_operator(): jnp.einsum('abcdeij,abcdejr->abcdir', local_links, columns, precision=lax...  8.81 us
    ppermute x4, waiting for transfers between devices, extended(): before = lax.ppermute(last, axis, up)  8.01 us
  transfers between devices with their start and end apart: 8, of which 4 were waited for; matrix products, arithmetic and copies ran while one was open for 0% of the time, Pallas kernels for 0%

commit v1 on v0

v1 whole, which is shorter than its diff:
```python
import functools

import jax
import jax.numpy as jnp
from jax import lax
from jax.experimental import pallas as pl
from jax.experimental.pallas import tpu as pltpu
from jax.sharding import PartitionSpec as P

NV = 32
POOL = 48
TB = 2
DOF = 12
HALF = DOF // 2
SITES = 256
RHS = 32
NC = 64
LANES = 2 * NC
CHUNKS = 4
ROWS = RHS // CHUNKS
SIDES = (
    ("gx", 1, 1),
    ("gx", -1, 2),
    ("gz", 1, 5),
    ("gz", -1, 6),
    ("gy", 1, 3),
    ("gy", -1, 4),
)
SEND_ORDER = (4, 5, 0, 1, 2, 3)
NEAR = 6
NT = (((1,), (1,)), ((), ()))
NN = (((1,), (0,)), ((), ()))


def dot(a, b, dims):
    return lax.dot_general(a, b, dims, preferred_element_type=jnp.float32)


def step_on(axis, step, size):
    return lax.rem(lax.axis_index(axis) + (step + size), size)


def picked(pick_ref, p, h):
    lane = lax.broadcasted_iota(jnp.int32, (2 * POOL, LANES), 1)
    row = lax.broadcasted_iota(jnp.int32, (2 * POOL, LANES), 0)
    wanted = jnp.zeros((2 * POOL, LANES), jnp.int32)
    for k in range(NV):
        wanted = jnp.where((lane & (NV - 1)) == k, pick_ref[k], wanted)
    part = row & 1
    hit = (row >> 1 == wanted) & (((lane >> 5) & 1) == h) & ((part ^ p) == lane >> 6)
    sign = jnp.where((part == 1) & (p == 0), -1.0, 1.0)
    return jnp.where(hit, sign, 0.0).astype(jnp.bfloat16)


def kernel(
    sizes,
    pick_ref,
    fine_ref,
    cand_ref,
    links_ref,
    corr_ref,
    err_ref,
    fine_v,
    cand_v,
    chosen_v,
    links_v,
    oper_v,
    rhs_v,
    mid_v,
    got_v,
    error_v,
    corr_v,
    in_sem,
    out_sem,
    send_sem,
    recv_sem,
):
    loads = []
    for t in range(TB):
        loads.append(pltpu.make_async_copy(cand_ref.at[t], cand_v.at[t], in_sem.at[2 * t]))
        loads.append(pltpu.make_async_copy(fine_ref.at[t], fine_v.at[t], in_sem.at[2 * t + 1]))
    loads.append(pltpu.make_async_copy(links_ref.at[lax.axis_index("gx")], links_v, in_sem.at[4]))
    for load in loads:
        load.start()

    barrier = pltpu.get_barrier_semaphore()
    for axis, step, _ in SIDES:
        pl.semaphore_signal(
            barrier,
            inc=1,
            device_id={axis: step_on(axis, step, sizes[axis])},
            device_id_type=pl.DeviceIdType.MESH,
        )

    def transfer(turn, chunk, side):
        axis, step, _ = SIDES[side]
        return pltpu.make_async_remote_copy(
            src_ref=(rhs_v, mid_v)[turn].at[chunk],
            dst_ref=got_v.at[turn, side, chunk],
            send_sem=send_sem.at[turn, chunk, side],
            recv_sem=recv_sem.at[turn, chunk, side],
            device_id={axis: step_on(axis, -step, sizes[axis])},
            device_id_type=pl.DeviceIdType.MESH,
        )

    select = [[picked(pick_ref, p, h) for h in range(2)] for p in range(2)]

    for t in range(TB):
        loads[2 * t].wait()
        loads[2 * t + 1].wait()
        total = jnp.zeros((RHS, LANES), jnp.float32)
        for h in range(2):
            some = range(h * HALF, (h + 1) * HALF)
            for a in some:
                chosen_v[t, a] = cand_v[t, :, a].reshape(2 * POOL, SITES)
            vectors = jnp.concatenate([chosen_v[t, a] for a in some], axis=1)
            field = jnp.concatenate([fine_v[t, :, a].reshape(2 * RHS, SITES) for a in some], axis=1)
            terms = dot(field, vectors, NT)
            high = terms.astype(jnp.bfloat16)
            rest = terms - high.astype(jnp.float32)
            low = rest.astype(jnp.bfloat16)
            lowest = (rest - low.astype(jnp.float32)).astype(jnp.bfloat16)
            for p in range(2):
                here = slice(p * RHS, (p + 1) * RHS)
                for piece in (high, low, lowest):
                    total = total + dot(piece[here], select[p][h], NN)
        for c in range(CHUNKS):
            rhs_v[c, t] = total[c * ROWS : (c + 1) * ROWS]

    pl.semaphore_wait(barrier, len(SIDES))
    for c in range(CHUNKS):
        for side in SEND_ORDER:
            transfer(0, c, side).start()

    loads[4].wait()
    lane = lax.broadcasted_iota(jnp.int32, (NC, LANES), 1)
    for t in range(TB):
        blocks = [links_v[t, 0], -(links_v[t, 7] + links_v[t, 8])]
        blocks = blocks + [-links_v[t, link] for _, _, link in SIDES]
        for i, block in enumerate(blocks):
            columns = slice(i * LANES, (i + 1) * LANES)
            oper_v[t, :NC, columns] = jnp.where(lane < NC, block, -block).astype(jnp.bfloat16)
            oper_v[t, NC:, columns] = pltpu.roll(block, NC, 1).astype(jnp.bfloat16)

    def image(turn, c):
        vector = (rhs_v, mid_v)[turn]
        own = [vector[c, t].astype(jnp.bfloat16) for t in range(TB)]
        parts = []
        for side in range(len(SIDES)):
            transfer(turn, c, side).wait_recv()
        for t in range(TB):
            row = [own[t], own[1 - t]]
            row = row + [got_v[turn, side, c, t].astype(jnp.bfloat16) for side in range(len(SIDES))]
            parts.append(dot(jnp.concatenate(row, axis=1), oper_v[t], NT))
        return parts

    for c in range(CHUNKS):
        found = image(0, c)
        for t in range(TB):
            mid_v[c, t] = 0.75 * rhs_v[c, t] - 0.25 * found[t]
        for side in SEND_ORDER:
            transfer(1, c, side).start()

    for c in range(CHUNKS):
        found = image(1, c)
        rows = slice(c * ROWS, (c + 1) * ROWS)
        for t in range(TB):
            error = 0.5 * (mid_v[c, t] + rhs_v[c, t] - found[t])
            error_v[t, rows] = error
            err_ref[t, 0, rows] = error[:, :NC]
            err_ref[t, 1, rows] = error[:, NC:]

    stores = []
    for t in range(TB):
        error_half = error_v[t].astype(jnp.bfloat16)
        for h in range(2):
            factor = jnp.concatenate([dot(error_half, select[q][h], NT) for q in range(2)], axis=0)
            factor = factor.astype(jnp.bfloat16)
            for a in range(h * HALF, (h + 1) * HALF):
                out = dot(factor, chosen_v[t, a], NN).astype(jnp.bfloat16)
                corr_v[t, 0, a] = out[:RHS]
                corr_v[t, 1, a] = out[RHS:]
        store = pltpu.make_async_copy(corr_v.at[t], corr_ref.at[t], out_sem.at[t])
        store.start()
        stores.append(store)

    for turn in range(2):
        for c in range(CHUNKS):
            for side in range(len(SIDES)):
                transfer(turn, c, side).wait_send()
    for store in stores:
        store.wait()


def on_device(sizes, fine_residual, candidates, vector_pick, coarse_links):
    fine = fine_residual[0, 0, 0]
    pool = jnp.swapaxes(candidates[0, 0, 0], 2, 3)
    links = coarse_links[:, 0, 0]
    hbm = pl.BlockSpec(memory_space=pltpu.HBM)
    sides = len(SIDES)
    correction, error = pl.pallas_call(
        functools.partial(kernel, sizes),
        out_shape=(
            jax.ShapeDtypeStruct((TB, 2, DOF, RHS, SITES), jnp.bfloat16),
            jax.ShapeDtypeStruct((TB, 2, RHS, NC), jnp.float32),
        ),
        in_specs=[pl.BlockSpec(memory_space=pltpu.SMEM), hbm, hbm, hbm],
        out_specs=(hbm, pl.BlockSpec(memory_space=pltpu.VMEM)),
        scratch_shapes=[
            pltpu.VMEM((TB, 2, DOF, RHS, SITES), jnp.bfloat16),
            pltpu.VMEM((TB, POOL, DOF, 2, SITES), jnp.bfloat16),
            pltpu.VMEM((TB, DOF, 2 * POOL, SITES), jnp.bfloat16),
            pltpu.VMEM((TB, 9, NC, LANES), jnp.float32),
            pltpu.VMEM((TB, LANES, 8 * LANES), jnp.bfloat16),
            pltpu.VMEM((CHUNKS, TB, ROWS, LANES), jnp.float32),
            pltpu.VMEM((CHUNKS, TB, ROWS, LANES), jnp.float32),
            pltpu.VMEM((2, sides, CHUNKS, TB, ROWS, LANES), jnp.float32),
            pltpu.VMEM((TB, RHS, LANES), jnp.float32),
            pltpu.VMEM((TB, 2, DOF, RHS, SITES), jnp.bfloat16),
            pltpu.SemaphoreType.DMA((5,)),
            pltpu.SemaphoreType.DMA((TB,)),
            pltpu.SemaphoreType.DMA((2, CHUNKS, sides)),
            pltpu.SemaphoreType.DMA((2, CHUNKS, sides)),
        ],
        compiler_params=pltpu.CompilerParams(
            collective_id=0, has_side_effects=True, vmem_limit_bytes=48 << 20
        ),
        name="coarse_correction",
    )(vector_pick, fine, pool, links)
    return (correction[None, None, None], jnp.swapaxes(error, 2, 3)[None, None, None])


def solution(mesh):
    placed = (
        P("gx", "gy", "gz", None, None, None, None, None),
        P("gx", "gy", "gz", None, None, None, None, None),
        P(),
        P(None, "gy", "gz", None, None, None, None),
    )
    return jax.shard_map(
        functools.partial(on_device, dict(mesh.shape)),
        mesh=mesh,
        in_specs=placed,
        out_specs=(
            P("gx", "gy", "gz", None, None, None, None, None),
            P("gx", "gy", "gz", None, None, None, None),
        ),
        check_vma=False,
    )
```

time: 135 us -> 53.7 us (0.40)
  the two profiles are of different devices: /device:TPU:1 before, /device:TPU:38 now
where the time goes in v1:
time: 53.7 us; the launch traced here: 53.5 us
  Pallas kernels  48.3 us (90%)
  local copies, waits for them, and re-layouts  4.56 us (8%)
  between operations  0.65 us (1%)
    pallas_call x1, Pallas kernels, on_device(): pl.pallas_call(functools.partial(kernel, sizes), out_shape=(jax.ShapeDtyp...  48.3 us
    unnamed x8, local copies, waits for them, and re-layouts  4.56 us

profile of v1, /device:TPU:38, one launch (start us, length us, event | category | flops | bytes accessed | tf_op | source)
XLA Modules:
  0.0 53.5 jit_solution(4873686687507072990)
XLA Ops:
  0.6 0.0 copy-start
  0.6 1.3 %copy-done = bf16[1,1,1,2,48,2,12,256]{7,5,6,4,3,2,1,0:T(2,128)(2,1)S(1)} copy-done((bf16[1,1,1,2,48,2,12,256]{7,5,6,4,3,2,1,0:T(2,128)(2,1)S(1)}, bf16[1,1,1,2,48,2,12,256]{7,5,6,4,3,2,1,0:T(2,128)(2,1)}, u32[]{:S(2)}) %copy-start) | copy-done | bytes 1179672
  1.9 0.0 copy-start.1
  1.9 1.1 %copy-done.1 = bf16[1,1,1,2,2,12,32,256]{7,6,5,4,3,2,1,0:T(8,128)(2,1)S(1)} copy-done((bf16[1,1,1,2,2,12,32,256]{7,6,5,4,3,2,1,0:T(8,128)(2,1)S(1)}, bf16[1,1,1,2,2,12,32,256]{7,6,5,4,3,2,1,0:T(8,128)(2,1)}, u32[]{:S(2)}) %copy-start.1) | copy-done | bytes 786456
  3.0 0.0 copy-start.2
  3.0 0.7 %copy-done.2 = s32[32]{0:T(128)S(1)} copy-done((s32[32]{0:T(128)S(1)}, s32[32]{0:T(128)}, u32[]{:S(2)}) %copy-start.2) | copy-done | bytes 152
  3.7 48.3 %coarse_correction.1 = (bf16[2,2,12,32,256]{4,3,2,1,0:T(8,128)(2,1)S(1)}, f32[2,2,32,64]{3,2,1,0:T(8,128)S(1)}) custom-call(s32[32]{0:T(128)S(1)} %copy-done.2, bf16[2,2,12,32,256]{4,3,2,1,0:T(8,128)(2,1)S(1)} %bitcast.11, bf16[2,48,12,2,256]{4,3,2,1,0:T(2,128)(2,1)S(1)} %bitcast.9, f32[8,2,9,64,128]{4,3,2,1,0:T(8,128)} %bitcast.13), custom_call_target="tpu_custom_call" | custom-call | tf_op jit(solution)/shard_map/coarse_correction/pallas_call | solution.py:201
  52.0 0.9 %copy.8 = bf16[1,1,1,2,2,12,32,256]{7,6,5,4,3,2,1,0:T(8,128)(2,1)} copy(bf16[1,1,1,2,2,12,32,256]{7,6,5,4,3,2,1,0:T(8,128)(2,1)S(1)} %bitcast.10) | data formatting | bytes 1572864
  52.9 0.6 %copy.9 = f32[1,1,1,2,2,64,32]{5,6,4,3,2,1,0:T(8,128)} copy(f32[1,1,1,2,2,64,32]{5,6,4,3,2,1,0:T(8,128)S(1)} %bitcast.12) | data formatting | bytes 65536
Async XLA Ops:
  0.6 1.3 %copy-start = (bf16[1,1,1,2,48,2,12,256]{7,5,6,4,3,2,1,0:T(2,128)(2,1)S(1)}, bf16[1,1,1,2,48,2,12,256]{7,5,6,4,3,2,1,0:T(2,128)(2,1)}, u32[]{:S(2)}) copy-start(bf16[1,1,1,2,48,2,12,256]{7,5,6,4,3,2,1,0:T(2,128)(2,1)} %param.5) | copy-start | bytes 3538948
  1.9 1.1 %copy-start.1 = (bf16[1,1,1,2,2,12,32,256]{7,6,5,4,3,2,1,0:T(8,128)(2,1)S(1)}, bf16[1,1,1,2,2,12,32,256]{7,6,5,4,3,2,1,0:T(8,128)(2,1)}, u32[]{:S(2)}) copy-start(bf16[1,1,1,2,2,12,32,256]{7,6,5,4,3,2,1,0:T(8,128)(2,1)} %param.4) | copy-start | bytes 2359300
  3.0 0.7 %copy-start.2 = (s32[32]{0:T(128)S(1)}, s32[32]{0:T(128)}, u32[]{:S(2)}) copy-start(s32[32]{0:T(128)} %pick_ref.1) | copy-start | bytes 388

commit v2 on v1

v2 whole, which is shorter than its diff:
```python
import functools

import jax
import jax.numpy as jnp
from jax import lax
from jax.experimental import pallas as pl
from jax.experimental.pallas import tpu as pltpu
from jax.sharding import PartitionSpec as P

NV = 32
POOL = 48
TB = 2
DOF = 12
HALF = DOF // 2
SITES = 256
RHS = 32
NC = 64
LANES = 2 * NC
ROWS = 16
UNITS = tuple((t, first) for t in range(TB) for first in range(0, RHS, ROWS))
SIDES = (
    ("gz", 1, 5),
    ("gz", -1, 6),
    ("gx", 1, 1),
    ("gx", -1, 2),
    ("gy", 1, 3),
    ("gy", -1, 4),
)
NEAR = (0, 1, 2, 3)
FAR = (4, 5)
NT = (((1,), (1,)), ((), ()))
NN = (((1,), (0,)), ((), ()))


def dot(a, b, dims):
    return lax.dot_general(a, b, dims, preferred_element_type=jnp.float32)


def step_on(axis, step, size):
    return lax.rem(lax.axis_index(axis) + (step + size), size)


def picked(pick, p, h):
    lane = lax.broadcasted_iota(jnp.int32, (2 * POOL, LANES), 1)
    row = lax.broadcasted_iota(jnp.int32, (2 * POOL, LANES), 0)
    wanted = jnp.concatenate([pick] * (LANES // NV), axis=1)
    part = row & 1
    hit = (row >> 1 == wanted) & (((lane >> 5) & 1) == h) & ((part ^ p) == lane >> 6)
    sign = jnp.where((part == 1) & (p == 0), -1.0, 1.0)
    return jnp.where(hit, sign, 0.0).astype(jnp.bfloat16)


def kernel(
    sizes,
    pick_ref,
    fine_ref,
    cand_ref,
    links_ref,
    err_ref,
    factor_ref,
    chosen_v,
    fine_v,
    cand_v,
    links_v,
    oper_v,
    rhs_v,
    mid_v,
    got_v,
    pick_v,
    in_sem,
    send_sem,
    recv_sem,
):
    barrier = pltpu.get_barrier_semaphore()
    for axis, step, _ in reversed(SIDES):
        pl.semaphore_signal(
            barrier,
            inc=1,
            device_id={axis: step_on(axis, step, sizes[axis])},
            device_id_type=pl.DeviceIdType.MESH,
        )

    loads = [pltpu.make_async_copy(pick_ref, pick_v, in_sem.at[5])]
    for t in range(TB):
        loads.append(pltpu.make_async_copy(cand_ref.at[t], cand_v.at[t], in_sem.at[2 * t]))
        loads.append(pltpu.make_async_copy(fine_ref.at[t], fine_v.at[t], in_sem.at[2 * t + 1]))
    loads.append(pltpu.make_async_copy(links_ref.at[lax.axis_index("gx")], links_v, in_sem.at[4]))

    for load in loads:
        load.start()

    def transfer(turn, unit, side):
        t, first = UNITS[unit]
        rows = pl.ds(first, ROWS)
        axis, step, _ = SIDES[side]
        return pltpu.make_async_remote_copy(
            src_ref=(rhs_v, mid_v)[turn].at[t, rows],
            dst_ref=got_v.at[turn, side, t, rows],
            send_sem=send_sem.at[turn, unit, side],
            recv_sem=recv_sem.at[turn, unit, side],
            device_id={axis: step_on(axis, -step, sizes[axis])},
            device_id_type=pl.DeviceIdType.MESH,
        )

    loads[0].wait()
    select = [[picked(pick_v[...], p, h) for h in range(2)] for p in range(2)]

    for t in range(TB):
        loads[2 * t + 1].wait()
        loads[2 * t + 2].wait()
        total = jnp.zeros((RHS, LANES), jnp.float32)
        for h in range(2):
            some = range(h * HALF, (h + 1) * HALF)
            for a in some:
                chosen_v[t, a] = cand_v[t, :, a].reshape(2 * POOL, SITES)
            vectors = jnp.concatenate([chosen_v[t, a] for a in some], axis=1)
            field = jnp.concatenate([fine_v[t, :, a].reshape(2 * RHS, SITES) for a in some], axis=1)
            terms = dot(field, vectors, NT)
            high = terms.astype(jnp.bfloat16)
            rest = terms - high.astype(jnp.float32)
            low = rest.astype(jnp.bfloat16)
            lowest = (rest - low.astype(jnp.float32)).astype(jnp.bfloat16)
            for p in range(2):
                here = slice(p * RHS, (p + 1) * RHS)
                for piece in (high, low, lowest):
                    total = total + dot(piece[here], select[p][h], NN)
        rhs_v[t] = total

    loads[5].wait()
    lane = lax.broadcasted_iota(jnp.int32, (NC, LANES), 1)
    for t in range(TB):
        blocks = [links_v[t, 0], -(links_v[t, 7] + links_v[t, 8])]
        blocks = blocks + [-links_v[t, link] for _, _, link in SIDES]
        for i, block in enumerate(blocks):
            signed = jnp.where(lane < NC, block, -block)
            turned = pltpu.roll(block, NC, 1)
            whole = jnp.concatenate([signed, turned], axis=0)
            oper_v[t, i * LANES : (i + 1) * LANES] = whole.T.astype(jnp.bfloat16)

    pl.semaphore_wait(barrier, len(SIDES))
    for unit in range(len(UNITS)):
        for side in FAR:
            transfer(0, unit, side).start()
        if unit:
            for side in NEAR:
                transfer(0, unit - 1, side).start()
    for side in NEAR:
        transfer(0, len(UNITS) - 1, side).start()

    def image(turn, unit):
        t, first = UNITS[unit]
        rows = pl.ds(first, ROWS)
        vector = (rhs_v, mid_v)[turn]
        total = jnp.zeros((ROWS, LANES), jnp.float32)
        parts = [vector[t, rows], vector[1 - t, rows]]
        column = 0
        for sides in (NEAR, FAR):
            for side in sides:
                transfer(turn, unit, side).wait_recv()
                parts.append(got_v[turn, side, t, rows])
            joined = jnp.concatenate([part.astype(jnp.bfloat16) for part in parts], axis=1)
            width = joined.shape[1]
            total = total + dot(joined, oper_v[t, column : column + width], NN)
            column = column + width
            parts = []
        return total

    for unit, (t, first) in enumerate(UNITS):
        rows = pl.ds(first, ROWS)
        mid_v[t, rows] = 0.75 * rhs_v[t, rows] - 0.25 * image(0, unit)
        for side in FAR + NEAR:
            transfer(1, unit, side).start()

    for unit, (t, first) in enumerate(UNITS):
        rows = pl.ds(first, ROWS)
        error = 0.5 * (mid_v[t, rows] + rhs_v[t, rows] - image(1, unit))
        err_ref[t, rows] = error
        error_half = error.astype(jnp.bfloat16)
        for h in range(2):
            for q in range(2):
                factor = dot(error_half, select[q][h], NT).astype(jnp.bfloat16)
                factor_ref[t, h, pl.ds(q * RHS + first, ROWS)] = factor

    for turn in range(2):
        for unit in range(len(UNITS)):
            for side in range(len(SIDES)):
                transfer(turn, unit, side).wait_send()


def prolong(error_ref, factor_ref, chosen_ref, corr_ref, err_ref, corr_v, err_v, sems):
    for t in range(TB):
        err_v[t, 0] = error_ref[t, :, :NC]
        err_v[t, 1] = error_ref[t, :, NC:]
    stores = [pltpu.make_async_copy(err_v, err_ref, sems.at[4])]
    stores[0].start()
    for t in range(TB):
        for h in range(2):
            for a in range(h * HALF, (h + 1) * HALF):
                out = dot(factor_ref[t, h], chosen_ref[t, a], NN).astype(jnp.bfloat16)
                corr_v[t, 0, a] = out[:RHS]
                corr_v[t, 1, a] = out[RHS:]
            some = pl.ds(h * HALF, HALF)
            store = pltpu.make_async_copy(
                corr_v.at[t, :, some], corr_ref.at[t, :, some], sems.at[2 * t + h]
            )
            store.start()
            stores.append(store)
    for store in stores:
        store.wait()


def on_device(sizes, fine_residual, candidates, vector_pick, coarse_links):
    fine = fine_residual[0, 0, 0]
    pool = jnp.swapaxes(candidates[0, 0, 0], 2, 3)
    links = coarse_links[:, 0, 0]
    hbm = pl.BlockSpec(memory_space=pltpu.HBM)
    sides = len(SIDES)
    error, factor, chosen = pl.pallas_call(
        functools.partial(kernel, sizes),
        out_shape=(
            pltpu.VMEM((TB, RHS, LANES), jnp.float32),
            pltpu.VMEM((TB, 2, 2 * RHS, 2 * POOL), jnp.bfloat16),
            pltpu.VMEM((TB, DOF, 2 * POOL, SITES), jnp.bfloat16),
        ),
        in_specs=[hbm] * 4,
        out_specs=(pl.BlockSpec(memory_space=pltpu.VMEM),) * 3,
        scratch_shapes=[
            pltpu.VMEM((TB, 2, DOF, RHS, SITES), jnp.bfloat16),
            pltpu.VMEM((TB, POOL, DOF, 2, SITES), jnp.bfloat16),
            pltpu.VMEM((TB, 9, NC, LANES), jnp.float32),
            pltpu.VMEM((TB, 8 * LANES, LANES), jnp.bfloat16),
            pltpu.VMEM((TB, RHS, LANES), jnp.float32),
            pltpu.VMEM((TB, RHS, LANES), jnp.float32),
            pltpu.VMEM((2, sides, TB, RHS, LANES), jnp.float32),
            pltpu.VMEM((1, NV), jnp.int32),
            pltpu.SemaphoreType.DMA((6,)),
            pltpu.SemaphoreType.DMA((2, len(UNITS), sides)),
            pltpu.SemaphoreType.DMA((2, len(UNITS), sides)),
        ],
        compiler_params=pltpu.CompilerParams(
            collective_id=0, has_side_effects=True, vmem_limit_bytes=48 << 20
        ),
        name="coarse_correction",
    )(*[pltpu.with_memory_space_constraint(x, pltpu.HBM) for x in (vector_pick[None], fine, pool, links)])
    vmem = pl.BlockSpec(memory_space=pltpu.VMEM)
    correction, error = pl.pallas_call(
        prolong,
        out_shape=(
            pltpu.HBM((TB, 2, DOF, RHS, SITES), jnp.bfloat16),
            pltpu.HBM((TB, 2, RHS, NC), jnp.float32),
        ),
        in_specs=[vmem] * 3,
        out_specs=(hbm, hbm),
        scratch_shapes=[
            pltpu.VMEM((TB, 2, DOF, RHS, SITES), jnp.bfloat16),
            pltpu.VMEM((TB, 2, RHS, NC), jnp.float32),
            pltpu.SemaphoreType.DMA((5,)),
        ],
        compiler_params=pltpu.CompilerParams(vmem_limit_bytes=32 << 20),
        name="prolong",
    )(*[pltpu.with_memory_space_constraint(x, pltpu.VMEM) for x in (error, factor, chosen)])
    return (correction[None, None, None], jnp.swapaxes(error, 2, 3)[None, None, None])


def solution(mesh):
    placed = (
        P("gx", "gy", "gz", None, None, None, None, None),
        P("gx", "gy", "gz", None, None, None, None, None),
        P(),
        P(None, "gy", "gz", None, None, None, None),
    )
    return jax.shard_map(
        functools.partial(on_device, dict(mesh.shape)),
        mesh=mesh,
        in_specs=placed,
        out_specs=(
            P("gx", "gy", "gz", None, None, None, None, None),
            P("gx", "gy", "gz", None, None, None, None),
        ),
        check_vma=False,
    )
```

time: 53.7 us -> 47.6 us (0.89)
  the two profiles are of different devices: /device:TPU:38 before, /device:TPU:34 now
where the time goes in v2:
time: 47.6 us; the launch traced here: 47.4 us
  Pallas kernels  46.8 us (98%)
  between operations  0.64 us (1%)
    pallas_call x1, Pallas kernels, on_device(): pl.pallas_call(functools.partial(kernel, sizes), out_shape=(pltpu.VMEM((T...  45.7 us
    pallas_call x1, Pallas kernels, on_device(): pl.pallas_call(prolong, out_shape=(pltpu.HBM((TB, 2, DOF, RHS, SITES), jn...  1.12 us

profile of v2, /device:TPU:34, one launch (start us, length us, event | category | flops | bytes accessed | tf_op | source)
XLA Modules:
  0.0 47.4 jit_solution(6891414392521767993)
XLA Ops:
  0.6 45.7 %coarse_correction.1 = (f32[2,32,128]{2,1,0:T(8,128)S(1)}, bf16[2,2,64,96]{3,2,1,0:T(8,128)(2,1)S(1)}, bf16[2,12,96,256]{3,2,1,0:T(8,128)(2,1)S(1)}) custom-call(s32[1,32]{1,0:T(1,128)} %bitcast.13, bf16[2,2,12,32,256]{4,3,2,1,0:T(8,128)(2,1)} %bitcast.12, bf16[2,48,12,2,256]{4,3,2,1,0:T(2,128)(2,1)} %bitcast.11, f32[8,2,9,64,128]{4,3,2,1,0:T(8,128)} %bitcast.10), custom_call_target="tpu_custom_call" | custom-call | tf_op jit(solution)/shard_map/coarse_correction/pallas_call | solution.py:218
  46.3 1.1 %prolong.1 = (bf16[2,2,12,32,256]{4,3,2,1,0:T(8,128)(2,1)}, f32[2,2,32,64]{3,2,1,0:T(8,128)}) custom-call(f32[2,32,128]{2,1,0:T(8,128)S(1)} %get-tuple-element.7.error_ref, bf16[2,2,64,96]{3,2,1,0:T(8,128)(2,1)S(1)} %get-tuple-element.8.factor_ref, bf16[2,12,96,256]{3,2,1,0:T(8,128)(2,1)S(1)} %get-tuple-element.9.chosen_ref), custom_call_target="tpu_custom_call" | custom-call | tf_op jit(solution)/shard_map/prolong/pallas_call | solution.py:246

commit v3 on v2

--- a/solution.py
+++ b/solution.py
@@ -26,6 +26,7 @@
     ("gy", 1, 3),
     ("gy", -1, 4),
 )
+LAST = len(UNITS) - 1
 NEAR = (0, 1, 2, 3)
 FAR = (4, 5)
 NT = (((1,), (1,)), ((), ()))
@@ -41,13 +42,13 @@
 
 
 def picked(pick, p, h):
-    lane = lax.broadcasted_iota(jnp.int32, (2 * POOL, LANES), 1)
-    row = lax.broadcasted_iota(jnp.int32, (2 * POOL, LANES), 0)
+    lane = lax.broadcasted_iota(jnp.int32, (LANES, LANES), 1)
+    row = lax.broadcasted_iota(jnp.int32, (LANES, LANES), 0)
     wanted = jnp.concatenate([pick] * (LANES // NV), axis=1)
     part = row & 1
     hit = (row >> 1 == wanted) & (((lane >> 5) & 1) == h) & ((part ^ p) == lane >> 6)
     sign = jnp.where((part == 1) & (p == 0), -1.0, 1.0)
-    return jnp.where(hit, sign, 0.0).astype(jnp.bfloat16)
+    return jnp.where(hit, sign, 0.0)
 
 
 def kernel(
@@ -63,10 +64,13 @@
     cand_v,
     links_v,
     oper_v,
+    oper_low_v,
     rhs_v,
     mid_v,
     got_v,
     pick_v,
+    select_v,
+    spread_v,
     in_sem,
     send_sem,
     recv_sem,
@@ -103,9 +107,14 @@
         )
 
     loads[0].wait()
-    select = [[picked(pick_v[...], p, h) for h in range(2)] for p in range(2)]
-
-    for t in range(TB):
+    for p in range(2):
+        for h in range(2):
+            matrix = picked(pick_v[...], p, h)
+            select_v[p, h] = matrix[: 2 * POOL].astype(jnp.bfloat16)
+            columns = slice((2 * p + h) * LANES, (2 * p + h + 1) * LANES)
+            spread_v[:, columns] = matrix.T.astype(jnp.bfloat16)
+
+    def restrict(t):
         loads[2 * t + 1].wait()
         loads[2 * t + 2].wait()
         total = jnp.zeros((RHS, LANES), jnp.float32)
@@ -123,29 +132,38 @@
             for p in range(2):
                 here = slice(p * RHS, (p + 1) * RHS)
                 for piece in (high, low, lowest):
-                    total = total + dot(piece[here], select[p][h], NN)
+                    total = total + dot(piece[here], select_v[p, h], NN)
         rhs_v[t] = total
 
-    loads[5].wait()
     lane = lax.broadcasted_iota(jnp.int32, (NC, LANES), 1)
-    for t in range(TB):
+
+    def build(t):
         blocks = [links_v[t, 0], -(links_v[t, 7] + links_v[t, 8])]
         blocks = blocks + [-links_v[t, link] for _, _, link in SIDES]
         for i, block in enumerate(blocks):
             signed = jnp.where(lane < NC, block, -block)
             turned = pltpu.roll(block, NC, 1)
             whole = jnp.concatenate([signed, turned], axis=0)
-            oper_v[t, i * LANES : (i + 1) * LANES] = whole.T.astype(jnp.bfloat16)
-
+            whole = whole.T
+            high = whole.astype(jnp.bfloat16)
+            rows = slice(i * LANES, (i + 1) * LANES)
+            oper_v[t, rows] = high
+            oper_low_v[t, rows] = (whole - high.astype(jnp.float32)).astype(jnp.bfloat16)
+
+    def begin(turn, unit):
+        for side in FAR + NEAR:
+            transfer(turn, unit, side).start()
+
+    restrict(0)
     pl.semaphore_wait(barrier, len(SIDES))
-    for unit in range(len(UNITS)):
-        for side in FAR:
-            transfer(0, unit, side).start()
-        if unit:
-            for side in NEAR:
-                transfer(0, unit - 1, side).start()
-    for side in NEAR:
-        transfer(0, len(UNITS) - 1, side).start()
+    begin(0, 0)
+    loads[5].wait()
+    build(0)
+    begin(0, 1)
+    restrict(1)
+    begin(0, 2)
+    build(1)
+    begin(0, 3)
 
     def image(turn, unit):
         t, first = UNITS[unit]
@@ -158,9 +176,13 @@
             for side in sides:
                 transfer(turn, unit, side).wait_recv()
                 parts.append(got_v[turn, side, t, rows])
-            joined = jnp.concatenate([part.astype(jnp.bfloat16) for part in parts], axis=1)
+            joined = jnp.concatenate(parts, axis=1)
+            high = joined.astype(jnp.bfloat16)
+            low = (joined - high.astype(jnp.float32)).astype(jnp.bfloat16)
             width = joined.shape[1]
-            total = total + dot(joined, oper_v[t, column : column + width], NN)
+            both = dot(jnp.concatenate([high, low], axis=0), oper_v[t, column : column + width], NN)
+            rest = dot(high, oper_low_v[t, column : column + width], NN)
+            total = total + (both[:ROWS] + both[ROWS:] + rest)
             column = column + width
             parts = []
         return total
@@ -168,23 +190,22 @@
     for unit, (t, first) in enumerate(UNITS):
         rows = pl.ds(first, ROWS)
         mid_v[t, rows] = 0.75 * rhs_v[t, rows] - 0.25 * image(0, unit)
-        for side in FAR + NEAR:
-            transfer(1, unit, side).start()
+        begin(1, unit)
 
     for unit, (t, first) in enumerate(UNITS):
         rows = pl.ds(first, ROWS)
+        if unit == LAST:
+            for turn in range(2):
+                for sent in range(len(UNITS)):
+                    for side in range(len(SIDES)):
+                        transfer(turn, sent, side).wait_send()
         error = 0.5 * (mid_v[t, rows] + rhs_v[t, rows] - image(1, unit))
         err_ref[t, rows] = error
-        error_half = error.astype(jnp.bfloat16)
+        factors = dot(error.astype(jnp.bfloat16), spread_v[...], NN).astype(jnp.bfloat16)
         for h in range(2):
             for q in range(2):
-                factor = dot(error_half, select[q][h], NT).astype(jnp.bfloat16)
-                factor_ref[t, h, pl.ds(q * RHS + first, ROWS)] = factor
-
-    for turn in range(2):
-        for unit in range(len(UNITS)):
-            for side in range(len(SIDES)):
-                transfer(turn, unit, side).wait_send()
+                column = (2 * q + h) * LANES
+                factor_ref[t, h, pl.ds(q * RHS + first, ROWS)] = factors[:, column : column + 2 * POOL]
 
 
 def prolong(error_ref, factor_ref, chosen_ref, corr_ref, err_ref, corr_v, err_v, sems):
@@ -229,10 +250,13 @@
             pltpu.VMEM((TB, POOL, DOF, 2, SITES), jnp.bfloat16),
             pltpu.VMEM((TB, 9, NC, LANES), jnp.float32),
             pltpu.VMEM((TB, 8 * LANES, LANES), jnp.bfloat16),
+            pltpu.VMEM((TB, 8 * LANES, LANES), jnp.bfloat16),
             pltpu.VMEM((TB, RHS, LANES), jnp.float32),
             pltpu.VMEM((TB, RHS, LANES), jnp.float32),
             pltpu.VMEM((2, sides, TB, RHS, LANES), jnp.float32),
             pltpu.VMEM((1, NV), jnp.int32),
+            pltpu.VMEM((2, 2, 2 * POOL, LANES), jnp.bfloat16),
+            pltpu.VMEM((LANES, 4 * LANES), jnp.bfloat16),
             pltpu.SemaphoreType.DMA((6,)),
             pltpu.SemaphoreType.DMA((2, len(UNITS), sides)),
             pltpu.SemaphoreType.DMA((2, len(UNITS), sides)),

time: 47.6 us -> 47.7 us (level)
  the two profiles are of different devices: /device:TPU:34 before, /device:TPU:32 now
where the time goes in v3:
time: 47.7 us; the launch traced here: 47.6 us
  Pallas kernels  46.9 us (98%)
  between operations  0.64 us (1%)
    pallas_call x1, Pallas kernels, on_device(): pl.pallas_call(functools.partial(kernel, sizes), out_shape=(pltpu.VMEM((T...  45.8 us
    pallas_call x1, Pallas kernels, on_device(): pl.pallas_call(prolong, out_shape=(pltpu.HBM((TB, 2, DOF, RHS, SITES), jn...  1.11 us

profile of v3, /device:TPU:32, one launch (start us, length us, event | category | flops | bytes accessed | tf_op | source)
XLA Modules:
  0.0 47.6 jit_solution(3623355243332120879)
XLA Ops:
  0.6 45.8 %coarse_correction.1 = (f32[2,32,128]{2,1,0:T(8,128)S(1)}, bf16[2,2,64,96]{3,2,1,0:T(8,128)(2,1)S(1)}, bf16[2,12,96,256]{3,2,1,0:T(8,128)(2,1)S(1)}) custom-call(s32[1,32]{1,0:T(1,128)} %bitcast.13, bf16[2,2,12,32,256]{4,3,2,1,0:T(8,128)(2,1)} %bitcast.12, bf16[2,48,12,2,256]{4,3,2,1,0:T(2,128)(2,1)} %bitcast.11, f32[8,2,9,64,128]{4,3,2,1,0:T(8,128)} %bitcast.10), custom_call_target="tpu_custom_call" | custom-call | tf_op jit(solution)/shard_map/coarse_correction/pallas_call | solution.py:239
  46.4 1.1 %prolong.1 = (bf16[2,2,12,32,256]{4,3,2,1,0:T(8,128)(2,1)}, f32[2,2,32,64]{3,2,1,0:T(8,128)}) custom-call(f32[2,32,128]{2,1,0:T(8,128)S(1)} %get-tuple-element.7.error_ref, bf16[2,2,64,96]{3,2,1,0:T(8,128)(2,1)S(1)} %get-tuple-element.8.factor_ref, bf16[2,12,96,256]{3,2,1,0:T(8,128)(2,1)S(1)} %get-tuple-element.9.chosen_ref), custom_call_target="tpu_custom_call" | custom-call | tf_op jit(solution)/shard_map/prolong/pallas_call | solution.py:270

commit v4 on v3

--- a/solution.py
+++ b/solution.py
@@ -64,7 +64,6 @@
     cand_v,
     links_v,
     oper_v,
-    oper_low_v,
     rhs_v,
     mid_v,
     got_v,
@@ -144,11 +143,7 @@
             signed = jnp.where(lane < NC, block, -block)
             turned = pltpu.roll(block, NC, 1)
             whole = jnp.concatenate([signed, turned], axis=0)
-            whole = whole.T
-            high = whole.astype(jnp.bfloat16)
-            rows = slice(i * LANES, (i + 1) * LANES)
-            oper_v[t, rows] = high
-            oper_low_v[t, rows] = (whole - high.astype(jnp.float32)).astype(jnp.bfloat16)
+            oper_v[t, i * LANES : (i + 1) * LANES] = whole.T.astype(jnp.bfloat16)
 
     def begin(turn, unit):
         for side in FAR + NEAR:
@@ -176,13 +171,9 @@
             for side in sides:
                 transfer(turn, unit, side).wait_recv()
                 parts.append(got_v[turn, side, t, rows])
-            joined = jnp.concatenate(parts, axis=1)
-            high = joined.astype(jnp.bfloat16)
-            low = (joined - high.astype(jnp.float32)).astype(jnp.bfloat16)
+            joined = jnp.concatenate([part.astype(jnp.bfloat16) for part in parts], axis=1)
             width = joined.shape[1]
-            both = dot(jnp.concatenate([high, low], axis=0), oper_v[t, column : column + width], NN)
-            rest = dot(high, oper_low_v[t, column : column + width], NN)
-            total = total + (both[:ROWS] + both[ROWS:] + rest)
+            total = total + dot(joined, oper_v[t, column : column + width], NN)
             column = column + width
             parts = []
         return total
@@ -249,7 +240,6 @@
             pltpu.VMEM((TB, 2, DOF, RHS, SITES), jnp.bfloat16),
             pltpu.VMEM((TB, POOL, DOF, 2, SITES), jnp.bfloat16),
             pltpu.VMEM((TB, 9, NC, LANES), jnp.float32),
-            pltpu.VMEM((TB, 8 * LANES, LANES), jnp.bfloat16),
             pltpu.VMEM((TB, 8 * LANES, LANES), jnp.bfloat16),
             pltpu.VMEM((TB, RHS, LANES), jnp.float32),
             pltpu.VMEM((TB, RHS, LANES), jnp.float32),

time: 47.7 us -> 47.4 us (level)
  the two profiles are of different devices: /device:TPU:32 before, /device:TPU:36 now
where the time goes in v4:
time: 47.4 us; the launch traced here: 47.2 us
  Pallas kernels  46.6 us (98%)
  between operations  0.64 us (1%)
    pallas_call x1, Pallas kernels, on_device(): pl.pallas_call(functools.partial(kernel, sizes), out_shape=(pltpu.VMEM((T...  45.5 us
    pallas_call x1, Pallas kernels, on_device(): pl.pallas_call(prolong, out_shape=(pltpu.HBM((TB, 2, DOF, RHS, SITES), jn...  1.12 us

profile of v4, /device:TPU:36, one launch (start us, length us, event | category | flops | bytes accessed | tf_op | source)
XLA Modules:
  0.0 47.2 jit_solution(10682738698886244193)
XLA Ops:
  0.6 45.5 %coarse_correction.1 = (f32[2,32,128]{2,1,0:T(8,128)S(1)}, bf16[2,2,64,96]{3,2,1,0:T(8,128)(2,1)S(1)}, bf16[2,12,96,256]{3,2,1,0:T(8,128)(2,1)S(1)}) custom-call(s32[1,32]{1,0:T(1,128)} %bitcast.13, bf16[2,2,12,32,256]{4,3,2,1,0:T(8,128)(2,1)} %bitcast.12, bf16[2,48,12,2,256]{4,3,2,1,0:T(2,128)(2,1)} %bitcast.11, f32[8,2,9,64,128]{4,3,2,1,0:T(8,128)} %bitcast.10), custom_call_target="tpu_custom_call" | custom-call | tf_op jit(solution)/shard_map/coarse_correction/pallas_call | solution.py:230
  46.1 1.1 %prolong.1 = (bf16[2,2,12,32,256]{4,3,2,1,0:T(8,128)(2,1)}, f32[2,2,32,64]{3,2,1,0:T(8,128)}) custom-call(f32[2,32,128]{2,1,0:T(8,128)S(1)} %get-tuple-element.7.error_ref, bf16[2,2,64,96]{3,2,1,0:T(8,128)(2,1)S(1)} %get-tuple-element.8.factor_ref, bf16[2,12,96,256]{3,2,1,0:T(8,128)(2,1)S(1)} %get-tuple-element.9.chosen_ref), custom_call_target="tpu_custom_call" | custom-call | tf_op jit(solution)/shard_map/prolong/pallas_call | solution.py:260

commit v5 on v3

--- a/solution.py
+++ b/solution.py
@@ -150,9 +150,19 @@
             oper_v[t, rows] = high
             oper_low_v[t, rows] = (whole - high.astype(jnp.float32)).astype(jnp.bfloat16)
 
-    def begin(turn, unit):
-        for side in FAR + NEAR:
-            transfer(turn, unit, side).start()
+    part = lax.rem(lax.axis_index("gy"), 4)
+
+    def urgent(turn, side):
+        if turn == 0:
+            return (part != 2, part != 2, part != 2, part != 2, part != 3, part != 4)[side]
+        return (part == 0, part == 0, part == 0, part == 0, part == 1, part == 3)[side]
+
+    def begin(turn, unit, now=True):
+        for side in FAR[::-1] + NEAR:
+
+            @pl.when(urgent(turn, side) if now else jnp.logical_not(urgent(turn, side)))
+            def _():
+                transfer(turn, unit, side).start()
 
     restrict(0)
     pl.semaphore_wait(barrier, len(SIDES))
@@ -164,42 +174,56 @@
     begin(0, 2)
     build(1)
     begin(0, 3)
-
-    def image(turn, unit):
+    for unit in range(len(UNITS)):
+        begin(0, unit, now=False)
+
+    def gathered(turn, unit, parts, sides, column):
         t, first = UNITS[unit]
         rows = pl.ds(first, ROWS)
+        for side in sides:
+            transfer(turn, unit, side).wait_recv()
+            parts = parts + [got_v[turn, side, t, rows]]
+        joined = jnp.concatenate(parts, axis=1)
+        high = joined.astype(jnp.bfloat16)
+        low = (joined - high.astype(jnp.float32)).astype(jnp.bfloat16)
+        here = slice(column, column + joined.shape[1])
+        both = dot(jnp.concatenate([high, low], axis=0), oper_v[t, here], NN)
+        return both[:ROWS] + both[ROWS:] + dot(high, oper_low_v[t, here], NN)
+
+    def near(turn, unit):
+        t, first = UNITS[unit]
+        rows = pl.ds(first, ROWS)
         vector = (rhs_v, mid_v)[turn]
-        total = jnp.zeros((ROWS, LANES), jnp.float32)
-        parts = [vector[t, rows], vector[1 - t, rows]]
-        column = 0
-        for sides in (NEAR, FAR):
-            for side in sides:
-                transfer(turn, unit, side).wait_recv()
-                parts.append(got_v[turn, side, t, rows])
-            joined = jnp.concatenate(parts, axis=1)
-            high = joined.astype(jnp.bfloat16)
-            low = (joined - high.astype(jnp.float32)).astype(jnp.bfloat16)
-            width = joined.shape[1]
-            both = dot(jnp.concatenate([high, low], axis=0), oper_v[t, column : column + width], NN)
-            rest = dot(high, oper_low_v[t, column : column + width], NN)
-            total = total + (both[:ROWS] + both[ROWS:] + rest)
-            column = column + width
-            parts = []
-        return total
-
+        return gathered(turn, unit, [vector[t, rows], vector[1 - t, rows]], NEAR, 0)
+
+    def far(turn, unit):
+        return gathered(turn, unit, [], FAR, (2 + len(NEAR)) * LANES)
+
+    ahead = near(0, 0)
     for unit, (t, first) in enumerate(UNITS):
         rows = pl.ds(first, ROWS)
-        mid_v[t, rows] = 0.75 * rhs_v[t, rows] - 0.25 * image(0, unit)
+        image = ahead
+        if unit < LAST:
+            ahead = near(0, unit + 1)
+        image = image + far(0, unit)
+        mid_v[t, rows] = 0.75 * rhs_v[t, rows] - 0.25 * image
         begin(1, unit)
-
+    for unit in range(len(UNITS)):
+        begin(1, unit, now=False)
+
+    ahead = near(1, 0)
     for unit, (t, first) in enumerate(UNITS):
         rows = pl.ds(first, ROWS)
-        if unit == LAST:
+        image = ahead
+        if unit < LAST:
+            ahead = near(1, unit + 1)
+        else:
             for turn in range(2):
                 for sent in range(len(UNITS)):
                     for side in range(len(SIDES)):
                         transfer(turn, sent, side).wait_send()
-        error = 0.5 * (mid_v[t, rows] + rhs_v[t, rows] - image(1, unit))
+        image = image + far(1, unit)
+        error = 0.5 * (mid_v[t, rows] + rhs_v[t, rows] - image)
         err_ref[t, rows] = error
         factors = dot(error.astype(jnp.bfloat16), spread_v[...], NN).astype(jnp.bfloat16)
         for h in range(2):

time: 47.7 us -> 47.6 us (level)
  the two profiles are of different devices: /device:TPU:32 before, /device:TPU:36 now
where the time goes in v5:
time: 47.6 us; the launch traced here: 47.5 us
  Pallas kernels  46.8 us (98%)
  between operations  0.64 us (1%)
    pallas_call x1, Pallas kernels, on_device(): pl.pallas_call(functools.partial(kernel, sizes), out_shape=(pltpu.VMEM((T...  45.7 us
    pallas_call x1, Pallas kernels, on_device(): pl.pallas_call(prolong, out_shape=(pltpu.HBM((TB, 2, DOF, RHS, SITES), jn...  1.12 us

profile of v5, /device:TPU:36, one launch (start us, length us, event | category | flops | bytes accessed | tf_op | source)
XLA Modules:
  0.0 47.5 jit_solution(8274746043269469808)
XLA Ops:
  0.6 45.7 %coarse_correction.1 = (f32[2,32,128]{2,1,0:T(8,128)S(1)}, bf16[2,2,64,96]{3,2,1,0:T(8,128)(2,1)S(1)}, bf16[2,12,96,256]{3,2,1,0:T(8,128)(2,1)S(1)}) custom-call(s32[1,32]{1,0:T(1,128)} %bitcast.13, bf16[2,2,12,32,256]{4,3,2,1,0:T(8,128)(2,1)} %bitcast.12, bf16[2,48,12,2,256]{4,3,2,1,0:T(2,128)(2,1)} %bitcast.11, f32[8,2,9,64,128]{4,3,2,1,0:T(8,128)} %bitcast.10), custom_call_target="tpu_custom_call" | custom-call | tf_op jit(solution)/shard_map/coarse_correction/pallas_call | solution.py:263
  46.3 1.1 %prolong.1 = (bf16[2,2,12,32,256]{4,3,2,1,0:T(8,128)(2,1)}, f32[2,2,32,64]{3,2,1,0:T(8,128)}) custom-call(f32[2,32,128]{2,1,0:T(8,128)S(1)} %get-tuple-element.7.error_ref, bf16[2,2,64,96]{3,2,1,0:T(8,128)(2,1)S(1)} %get-tuple-element.8.factor_ref, bf16[2,12,96,256]{3,2,1,0:T(8,128)(2,1)S(1)} %get-tuple-element.9.chosen_ref), custom_call_target="tpu_custom_call" | custom-call | tf_op jit(solution)/shard_map/prolong/pallas_call | solution.py:294
